TPU v7x, 32 devices: a whole 2x2x4 slice. The times are simulated.
32 devices in a mesh: batch: 16 (over z, y, core), coef: 2 (over x).
Axes of the slice: x: 2, y: 2, z: 4, core: 2. Of those that a mesh axis runs over, the one named last changes fastest.
Arguments:
- jac_blocks: bfloat16 [128, 2, 2, 128, 128], P(('batch', 'coef')), may hold values from -0.52734375 to 0.52734375
- col_blocks: int32 [2, 128, 2], P('coef', 'batch'), may hold values from 0 to 15, all different within a row; in each aligned block of 8 rows (0 to 7, 8 to 15, ..., all dimensions but the last counted through in order) at most 2 rows name the same one
- residual: float32 [128, 128], P('batch'), may hold values from -6 to 6
- run_of_half: int32 [256], P('batch'), may hold values from 0 to 255, each once
- run_scale: bfloat16 [256], replicated, may hold values from 0.25 to 4
Outputs:
- diag_blocks: float32 [2, 16, 128, 128], P('coef', 'batch')
- gradient: float32 [2, 16, 128], P('coef', 'batch')
Inputs may be any that keep to these rules, and one draw needn't show every extreme that they name: `col_blocks`: the 2 column blocks of one row block in one group differ. For each group, among the row blocks of one batch index (aligned blocks of the row-block dimension), no column block is named more than 2 times, a bound that some block reaches. `run_of_half`: every run appears exactly once.
All inputs are finite; a program needn't handle non-finite values.
Results may differ from a plain program's by a relative error of at most 0.00043.
Values may be sent and summed in bfloat16 or wider, within the bound.
A program may use at most 64 MiB of HBM per device.

v0:
```python
import jax
import jax.numpy as jnp
from jax import lax
from jax.sharding import PartitionSpec as P

BS = 128
PAIR = 2


def shards(jac_blocks, col_blocks, residual, run_of_half, run_scale):
    width = lax.axis_size("batch")
    myself = lax.axis_index("batch")
    moved = lax.all_to_all(jac_blocks, "coef", split_axis=1, concat_axis=0, tiled=True)
    items = moved.reshape(-1, BS, BS)
    targets = col_blocks.reshape(-1)
    scale_rows = run_scale.astype(jnp.float32)[run_of_half].reshape(-1, 2)
    weights = jnp.repeat(scale_rows, BS // 2, axis=1)
    item_w = jnp.repeat(weights, PAIR, axis=0)
    item_res = jnp.repeat(residual, PAIR, axis=0)
    onehot = (targets[:, None] == jnp.arange(width, dtype=jnp.int32)[None, :]).astype(jnp.float32)
    gterms = jnp.einsum(
        "iak,ia->ik", items.astype(jnp.float32), item_w * item_res, precision=lax.Precision.HIGHEST
    )
    gpart = jnp.einsum("il,ik->lk", onehot, gterms, precision=lax.Precision.HIGHEST)
    gtotal = lax.psum(gpart, "batch")
    gradient = lax.dynamic_slice_in_dim(gtotal, myself, 1, 0).reshape(1, 1, BS)
    weighted = (items.astype(jnp.float32) * item_w[:, :, None]).astype(jnp.bfloat16)
    products = lax.dot_general(
        items, weighted, (((1,), (1,)), ((0,), (0,))), preferred_element_type=jnp.float32
    )
    diag = lax.psum_scatter(
        jnp.einsum("il,ikb->lkb", onehot, products, precision=lax.Precision.HIGHEST),
        "batch",
        scatter_dimension=0,
        tiled=True,
    )
    return (diag.reshape(1, 1, BS, BS), gradient)


def solution(mesh):
    in_specs = (
        P(("batch", "coef"), None, None, None, None),
        P("coef", "batch", None),
        P("batch", None),
        P("batch"),
        P(),
    )
    out_specs = (P("coef", "batch", None, None), P("coef", "batch", None))
    return jax.shard_map(shards, mesh=mesh, in_specs=in_specs, out_specs=out_specs, check_vma=False)
```

profile of v0, /device:TPU:0, one launch (start us, length us, event | category | flops | bytes accessed | tf_op | source)
XLA Modules:
  0.0 90.3 jit_solution(8798194722086360847)
XLA Ops:
  7.2 1.9 %copy.11 = bf16[4,2,2,128,128]{4,3,2,0,1:T(8,128)(2,1)} copy(bf16[4,2,2,128,128]{4,3,2,1,0:T(8,128)(2,1)} %param.5) | data formatting | bytes 1048576 | tf_op args[0]
  9.0 0.0 copy-start.2
  9.0 4.3 %all-to-all-start = ((bf16[4,2,2,128,128]{4,3,2,0,1:T(8,128)(2,1)}), bf16[4,2,2,128,128]{4,3,2,0,1:T(8,128)(2,1)S(1)}, u32[]{:S(2)}, u32[]{:S(2)}) async-start(bf16[4,2,2,128,128]{4,3,2,0,1:T(8,128)(2,1)} %copy.11), calls=%async_computation | async-start | bytes 1048576 | tf_op jit(solution)/shard_map/all_to_all | solution.py:13
  13.4 0.0 copy-start.3
  13.4 0.0 reduce-scatter.2.cloned.1.call-start
  13.4 0.0 copy-done.2
  13.4 0.6 copy-done.3
  14.1 0.7 gather_fusion
  14.7 0.1 reshape.27
  14.8 0.1 broadcast_in_dim.14
  14.9 0.0 copy-start.1
  14.9 0.1 reshape.28
  15.0 0.6 copy-done.1
  15.6 0.1 copy.10
  15.6 0.1 eq.15
  15.7 6.4 %all-to-all-done = bf16[4,2,2,128,128]{4,3,2,0,1:T(8,128)(2,1)S(1)} async-done(((bf16[4,2,2,128,128]{4,3,2,0,1:T(8,128)(2,1)}), bf16[4,2,2,128,128]{4,3,2,0,1:T(8,128)(2,1)S(1)}, u32[]{:S(2)}, u32[]{:S(2)}) %all-to-all-start) | async-done | bytes 524320 | tf_op jit(solution)/shard_map/all_to_all | solution.py:13
  22.1 0.8 convolution_bitcast_fusion
  22.9 0.5 copy.13
  23.4 0.6 fusion.3
  24.0 1.3 %copy.14 = f32[16,128,128]{2,1,0:T(8,128)} copy(f32[16,128,128]{2,0,1:T(8,128)S(1)} %fusion.3) | data formatting | bytes 2097152 | tf_op jit(solution)/shard_map/il,ikb->lkb/dot_general | solution.py:32
  25.3 0.0 reduce-scatter.2.cloned.1.call-update
  25.3 0.0 copy-start
  25.3 0.7 copy-done
  26.0 0.5 fusion.7
  26.5 0.1 fusion.1
  26.6 33.5 %psum.7 = f32[16,128]{1,0:T(8,128)S(1)} all-reduce(f32[16,128]{1,0:T(8,128)S(1)} %fusion.1), channel_id=1, replica_groups=mesh['batch'=16,'coef'=2] {'batch'}, use_global_device_ids=true, to_apply=%region_1.0 | all-reduce | flops 2048 | bytes 16384 | tf_op jit(solution)/shard_map/psum | solution.py:25
  60.1 0.5 dynamic-slice_bitcast_fusion
  60.7 22.8 %reduce-scatter.2.cloned.1.call-done = f32[1,128,128]{2,1,0:T(8,128)} async-done(((f32[16,128,128]{2,1,0:T(8,128)}), f32[1,128,128]{2,1,0:T(8,128)}) %reduce-scatter.2.cloned.1.call-update) | async-done | bytes 65552 | tf_op jit(solution)/shard_map/reduce_scatter | solution.py:31
  (6 shorter events, 0.0 us)
Async XLA Ops:
  9.0 4.3 %copy-start.2 = (bf16[256]{0:T(256)(128)(2,1)S(1)}, bf16[256]{0:T(256)(128)(2,1)}, u32[]{:S(2)}) copy-start(bf16[256]{0:T(256)(128)(2,1)} %param.9) | copy-start | bytes 1540
  9.0 13.1 %all-to-all-start = ((bf16[4,2,2,128,128]{4,3,2,0,1:T(8,128)(2,1)}), bf16[4,2,2,128,128]{4,3,2,0,1:T(8,128)(2,1)S(1)}, u32[]{:S(2)}, u32[]{:S(2)}) async-start(bf16[4,2,2,128,128]{4,3,2,0,1:T(8,128)(2,1)} %copy.11), calls=%async_computation | async-start | bytes 1048576 | tf_op jit(solution)/shard_map/all_to_all | solution.py:13
  13.4 0.7 copy-start.3
  13.4 70.0 %reduce-scatter.2.cloned.1.call-start = ((), (), s32[]{:S(2)}) async-start(), calls=%async_computation.2 | async-start | bytes 1114112 | tf_op jit(solution)/shard_map/reduce_scatter | solution.py:31
  14.9 0.7 copy-start.1
  25.3 0.7 copy-start
Sparse Core Ops, SparseCore 0:
  25.4 57.9 reduce-scatter.1
where the time goes:
time: 90.6 us; the launch traced here: 90.3 us
  blocking collectives  33.5 us (37%)
  waiting for transfers between devices  29.2 us (32%)
  between operations  14.1 us (16%)
  local copies, waits for them, and re-layouts  7.19 us (8%)
  starting transfers between devices  4.34 us (5%)
  matrix products  2.01 us (2%)
    psum x1, blocking collectives, shards(): gtotal = lax.psum(gpart, 'batch')  33.5 us
    reduce_scatter x1, waiting for transfers between devices, shards(): lax.psum_scatter(jnp.einsum('il,ikb->lkb', onehot, products, precision=la...  22.8 us
    all_to_all x1, waiting for transfers between devices, shards(): lax.all_to_all(jac_blocks, 'coef', split_axis=1, concat_axis=0, tiled=True)  6.38 us
    all_to_all x1, starting transfers between devices, shards(): lax.all_to_all(jac_blocks, 'coef', split_axis=1, concat_axis=0, tiled=True)  4.34 us
    unnamed x10, local copies, waits for them, and re-layouts  3.9 us
  transfers between devices with their start and end apart: 2, of which 2 were waited for; matrix products, arithmetic and copies ran while one was open for 2% of the time, Pallas kernels for 0%

commit v1 on v0

v1 whole, which is shorter than its diff:
```python
import functools

import jax
import jax.numpy as jnp
from jax import lax
from jax.experimental import pallas as pl
from jax.experimental.pallas import tpu as pltpu
from jax.sharding import PartitionSpec as P

BS = 128
HALF = BS // 2
PAIR = 2
ROWS = BS + 8
STEPS = 32766.0
MESH = pl.DeviceIdType.MESH


def kernel(
    n_batch, n_coef, r_dev,
    jac, targets, residual, runs, scale, diag, gradient,
    items, prods, weights, firsts, seconds,
    from_twin, to_twin, packed, sides, got_packed, got_sides,
    own_sem, jac_send, jac_recv, twin_send, twin_recv, send_sem, recv_sem, side_send, side_recv,
):
    b, c = lax.axis_index("batch"), lax.axis_index("coef")
    chips = n_batch // 2
    core, chip = lax.rem(b, 2), lax.div(b, 2)
    twin = b + 1 - 2 * core
    rows = r_dev * n_coef
    n_items = rows * PAIR

    own = pltpu.make_async_copy(jac.at[:, c], items.at[c], own_sem)
    own.start()

    barrier = pltpu.get_barrier_semaphore()
    for k in range(1, n_coef):
        pl.semaphore_signal(barrier, inc=1, device_id=(b, lax.rem(c + k, n_coef)), device_id_type=MESH)
    pl.semaphore_signal(barrier, inc=1, device_id=(twin, c), device_id_type=MESH)
    for k in range(1, chips):
        pl.semaphore_signal(
            barrier, inc=1, device_id=(2 * lax.rem(chip + k, chips) + core, c), device_id_type=MESH
        )
    pl.semaphore_wait(barrier, n_coef + chips - 1)

    def jac_copy(k, r):
        peer = lax.rem(c + k, n_coef)
        return pltpu.make_async_remote_copy(
            src_ref=jac.at[r, peer], dst_ref=items.at[c, r],
            send_sem=jac_send.at[k, r], recv_sem=jac_recv.at[k, r],
            device_id=(b, peer), device_id_type=MESH,
        )

    def jac_arrival(k, r):
        source = lax.rem(c + n_coef - k, n_coef)
        return pltpu.make_async_remote_copy(
            src_ref=jac.at[r, source], dst_ref=items.at[source, r],
            send_sem=jac_send.at[k, r], recv_sem=jac_recv.at[k, r],
            device_id=(b, source), device_id_type=MESH,
        )

    for k in range(1, n_coef):
        for r in range(r_dev):
            jac_copy(k, r).start()

    n_runs = scale.shape[1]
    halves = 2 * rows
    along = jnp.broadcast_to(runs[...].astype(jnp.float32), (halves, halves))
    across = lax.broadcasted_iota(jnp.int32, (halves, halves), 0)
    beside = lax.broadcasted_iota(jnp.int32, (halves, halves), 1)
    run = jnp.sum(jnp.where(across == beside, along, 0.0), axis=1, keepdims=True).astype(jnp.int32)
    hot = lax.broadcasted_iota(jnp.int32, (halves, n_runs), 1) == run
    table = jnp.broadcast_to(scale[...].astype(jnp.float32), (halves, n_runs))
    picked = jnp.sum(jnp.where(hot, table, 0.0), axis=1, keepdims=True)
    weights[...] = jnp.broadcast_to(picked, (halves, BS))

    prods[n_items] = jnp.zeros((ROWS, BS), jnp.float32)

    def find(l, _):
        first, second = jnp.int32(n_items), jnp.int32(n_items)
        for i in range(n_items):
            hit = targets[i] == l
            second = jnp.where(hit, first, second)
            first = jnp.where(hit, i, first)
        firsts[l] = first
        seconds[l] = second
        return 0

    lax.fori_loop(0, n_batch, find, 0)

    lane = lax.broadcasted_iota(jnp.int32, (1, BS), 1)
    sub = lax.broadcasted_iota(jnp.int32, (16, BS), 0)

    def multiply(source, r):
        row = source * r_dev + r
        top = weights[pl.ds(2 * row, 1), :]
        low = weights[pl.ds(2 * row + 1, 1), :]
        scaled = jnp.where(lane < HALF, top, low) * residual[pl.ds(row, 1), :]
        part0 = scaled.astype(jnp.bfloat16).astype(jnp.float32)
        part1 = (scaled - part0).astype(jnp.bfloat16).astype(jnp.float32)
        part2 = scaled - part0 - part1
        parts = jnp.where(sub == 0, part0, jnp.where(sub == 1, part1, jnp.where(sub == 2, part2, 0.0)))
        parts = parts.astype(jnp.bfloat16)
        for s in range(PAIR):
            block = items[source, r, s]
            wide = block.astype(jnp.float32)
            weighted = jnp.concatenate([wide[:HALF] * top, wide[HALF:] * low], axis=0).astype(jnp.bfloat16)
            slot = row * PAIR + s
            prods[slot, 0:BS, :] = lax.dot_general(
                block, weighted, (((0,), (0,)), ((), ())), preferred_element_type=jnp.float32
            )
            terms = jnp.dot(parts, block, preferred_element_type=jnp.float32)
            prods[slot, BS:ROWS, :] = terms[0:8] + terms[8:16]

    own.wait()
    for r in range(r_dev):
        multiply(c, r)
    for k in range(1, n_coef):
        for r in range(r_dev):
            jac_arrival(k, r).wait_recv()
            multiply(lax.rem(c + n_coef - k, n_coef), r)

    def partial(l):
        return prods[firsts[l]] + prods[seconds[l]]

    def twin_copy(d):
        return pltpu.make_async_remote_copy(
            src_ref=to_twin.at[d], dst_ref=from_twin.at[d],
            send_sem=twin_send.at[d], recv_sem=twin_recv.at[d],
            device_id=(twin, c), device_id_type=MESH,
        )

    def to_other_core(i, _):
        d = lax.rem(i + 1, chips)
        to_twin[d] = partial(2 * lax.rem(chip + d, chips) + 1 - core)
        twin_copy(d).start()
        return 0

    lax.fori_loop(0, chips, to_other_core, 0)

    def block_copy(d):
        peer = 2 * lax.rem(chip + d, chips) + core
        return pltpu.make_async_remote_copy(
            src_ref=packed.at[d], dst_ref=got_packed.at[d],
            send_sem=send_sem.at[d], recv_sem=recv_sem.at[d],
            device_id=(peer, c), device_id_type=MESH,
        )

    def side_copy(d):
        peer = 2 * lax.rem(chip + d, chips) + core
        return pltpu.make_async_remote_copy(
            src_ref=sides.at[d], dst_ref=got_sides.at[d],
            send_sem=side_send.at[d], recv_sem=side_recv.at[d],
            device_id=(peer, c), device_id_type=MESH,
        )

    sub8 = lax.broadcasted_iota(jnp.int32, (8, BS), 0)

    def to_owner(d, _):
        mine = partial(2 * lax.rem(chip + d, chips) + core)
        twin_copy(d).wait_recv()
        total = mine + from_twin[d]
        block = total[0:BS]
        largest = jnp.maximum(jnp.max(jnp.abs(block), axis=0, keepdims=True), 2e-34)
        packed[d] = jnp.round(block * (STEPS / largest)).astype(jnp.int32).astype(jnp.int16)
        grad = jnp.sum(total[BS:ROWS], axis=0, keepdims=True)
        sides[d] = jnp.where(sub8 == 0, grad, jnp.broadcast_to(largest * (1.0 / STEPS), (8, BS)))
        block_copy(d).start()
        side_copy(d).start()
        return 0

    lax.fori_loop(1, chips, to_owner, 0)

    mine = partial(b)
    twin_copy(0).wait_recv()
    mine = mine + from_twin[0]
    diag[0, 0] = mine[0:BS]
    gradient[0] = jnp.sum(mine[BS:ROWS], axis=0, keepdims=True)

    def collect(d, _):
        side_copy(d).wait_recv()
        block_copy(d).wait_recv()
        side = got_sides[d]
        diag[0, 0] += got_packed[d].astype(jnp.int32).astype(jnp.float32) * side[1:2]
        gradient[0] += side[0:1]
        return 0

    lax.fori_loop(1, chips, collect, 0)

    for k in range(1, n_coef):
        for r in range(r_dev):
            jac_copy(k, r).wait_send()

    def finish(d, _):
        twin_copy(d).wait_send()
        return 0

    lax.fori_loop(0, chips, finish, 0)

    def finish_owner(d, _):
        side_copy(d).wait_send()
        block_copy(d).wait_send()
        return 0

    lax.fori_loop(1, chips, finish_owner, 0)


def shards(jac_blocks, col_blocks, residual, run_of_half, run_scale):
    n_batch, n_coef = lax.axis_size("batch"), lax.axis_size("coef")
    r_dev = jac_blocks.shape[0]
    rows = r_dev * n_coef
    n_items = rows * PAIR
    chips = n_batch // 2
    vmem = pl.BlockSpec(memory_space=pltpu.VMEM)
    diag, gradient = pl.pallas_call(
        functools.partial(kernel, n_batch, n_coef, r_dev),
        out_shape=(
            jax.ShapeDtypeStruct((1, 1, BS, BS), jnp.float32),
            jax.ShapeDtypeStruct((1, 1, BS), jnp.float32),
        ),
        in_specs=[
            pl.BlockSpec(memory_space=pl.ANY),
            pl.BlockSpec(memory_space=pltpu.SMEM),
            vmem, vmem, vmem,
        ],
        out_specs=(vmem, vmem),
        scratch_shapes=[
            pltpu.VMEM((n_coef, r_dev, PAIR, BS, BS), jnp.bfloat16),
            pltpu.VMEM((n_items + 1, ROWS, BS), jnp.float32),
            pltpu.VMEM((2 * rows, BS), jnp.float32),
            pltpu.SMEM((n_batch,), jnp.int32),
            pltpu.SMEM((n_batch,), jnp.int32),
            pltpu.VMEM((chips, ROWS, BS), jnp.float32),
            pltpu.VMEM((chips, ROWS, BS), jnp.float32),
            pltpu.VMEM((chips, BS, BS), jnp.int16),
            pltpu.VMEM((chips, 8, BS), jnp.float32),
            pltpu.VMEM((chips, BS, BS), jnp.int16),
            pltpu.VMEM((chips, 8, BS), jnp.float32),
            pltpu.SemaphoreType.DMA,
            pltpu.SemaphoreType.DMA((n_coef, r_dev)),
            pltpu.SemaphoreType.DMA((n_coef, r_dev)),
            pltpu.SemaphoreType.DMA((chips,)),
            pltpu.SemaphoreType.DMA((chips,)),
            pltpu.SemaphoreType.DMA((chips,)),
            pltpu.SemaphoreType.DMA((chips,)),
            pltpu.SemaphoreType.DMA((chips,)),
            pltpu.SemaphoreType.DMA((chips,)),
        ],
        compiler_params=pltpu.CompilerParams(
            collective_id=0, has_side_effects=True, vmem_limit_bytes=40 * 1024 * 1024
        ),
    )(
        jac_blocks,
        col_blocks.reshape(-1),
        residual,
        run_of_half.reshape(1, -1),
        run_scale.reshape(1, -1),
    )
    return diag, gradient


def solution(mesh):
    in_specs = (
        P(("batch", "coef"), None, None, None, None),
        P("coef", "batch", None),
        P("batch", None),
        P("batch"),
        P(),
    )
    out_specs = (P("coef", "batch", None, None), P("coef", "batch", None))
    return jax.shard_map(shards, mesh=mesh, in_specs=in_specs, out_specs=out_specs, check_vma=False)
```

time: 90.6 us -> 26.6 us (0.29)
  blocking collectives: 33.5 us -> 0 us
  waiting for transfers between devices: 29.2 us -> 0 us
  Pallas kernels: 0 us -> 21.4 us
  between operations: 14.1 us -> 0.65 us
  starting transfers between devices: 4.34 us -> 0 us
  local copies, waits for them, and re-layouts: 7.19 us -> 4.25 us
  matrix products: 2.01 us -> 0 us
    psum x1 -> x0, blocking collectives: 33.5 us -> none  [shards(): gtotal = lax.psum(gpart, 'batch')]
    reduce_scatter x1 -> x0, waiting for transfers between devices: 22.8 us -> none  [shards(): lax.psum_scatter(jnp.einsum('il,ikb->lkb', onehot, products, precision=la...]
    pallas_call x0 -> x1, Pallas kernels: none -> 21.4 us  [shards(): pl.pallas_call(functools.partial(kernel, n_batch, n_coef, r_dev), out_sha...]
    all_to_all x1 -> x0, waiting for transfers between devices: 6.38 us -> none  [shards(): lax.all_to_all(jac_blocks, 'coef', split_axis=1, concat_axis=0, tiled=True)]
    all_to_all x1 -> x0, starting transfers between devices: 4.34 us -> none  [shards(): lax.all_to_all(jac_blocks, 'coef', split_axis=1, concat_axis=0, tiled=True)]
    dot_general x4 -> x0, matrix products: 2.01 us -> none  [the longest x1 0.76 us: shards(): lax.dot_general(items, weighted, (((1,), (1,)), ((0,), (0,))), preferred_...]
    dot_general x2 -> x0, local copies, waits for them, and re-layouts: 1.78 us -> none  [the longest x1 1.29 us: shards(): jnp.einsum('il,ikb->lkb', onehot, products, precision=lax.Precision.HIGHEST)]
    unnamed x10 -> x13, local copies, waits for them, and re-layouts: 3.9 us -> 4.16 us
  transfers between devices with their start and end apart: 2 -> 0, of which waited for: 2 -> 0; matrix products, arithmetic and copies ran while one was open for 2% -> 0% of each run, Pallas kernels for 0% -> 0%
where the time goes in v1:
time: 26.6 us; the launch traced here: 26.3 us
  Pallas kernels  21.4 us (80%)
  local copies, waits for them, and re-layouts  4.25 us (16%)
  between operations  0.65 us (2%)
    pallas_call x1, Pallas kernels, shards(): pl.pallas_call(functools.partial(kernel, n_batch, n_coef, r_dev), out_sha...  21.4 us
    unnamed x13, local copies, waits for them, and re-layouts  4.16 us

profile of v1, /device:TPU:0, one launch (start us, length us, event | category | flops | bytes accessed | tf_op | source)
XLA Modules:
  0.0 26.3 jit_solution(17218429244202577254)
XLA Ops:
  0.6 0.0 copy-start.4
  0.6 0.6 %copy-done.4 = bf16[256]{0:T(256)(128)(2,1)S(1)} copy-done((bf16[256]{0:T(256)(128)(2,1)S(1)}, bf16[256]{0:T(256)(128)(2,1)}, u32[]{:S(2)}) %copy-start.4) | copy-done | bytes 536
  1.3 0.0 copy-start.3
  1.3 0.7 %copy-done.3 = s32[1,8,2]{1,2,0:T(2,128)S(1)} copy-done((s32[1,8,2]{1,2,0:T(2,128)S(1)}, s32[1,8,2]{1,2,0:T(2,128)}, u32[]{:S(2)}) %copy-start.3) | copy-done | bytes 88
  2.0 0.0 copy-start.1
  2.0 0.1 copy.8
  2.0 0.0 copy-start.2
  2.1 0.1 reshape.13.targets
  2.1 0.5 %copy-done.1 = f32[8,128]{1,0:T(8,128)S(1)} copy-done((f32[8,128]{1,0:T(8,128)S(1)}, f32[8,128]{1,0:T(8,128)}, u32[]{:S(2)}) %copy-start.1) | copy-done | bytes 4120
  2.7 0.1 copy-done.2
  2.7 0.0 copy-start
  2.7 1.0 %copy-done = bf16[4,2,2,128,128]{4,3,2,1,0:T(8,128)(2,1)S(1)} copy-done((bf16[4,2,2,128,128]{4,3,2,1,0:T(8,128)(2,1)S(1)}, bf16[4,2,2,128,128]{4,3,2,1,0:T(8,128)(2,1)}, u32[]{:S(2)}) %copy-start) | copy-done | bytes 524312
  3.7 21.4 %shard_map.68 = (f32[1,1,128,128]{3,2,1,0:T(8,128)S(1)}, f32[1,1,128]{2,1,0:T(1,128)S(1)}) custom-call(bf16[4,2,2,128,128]{4,3,2,1,0:T(8,128)(2,1)S(1)} %copy-done, s32[16]{0:T(128)S(1)} %reshape.13.targets, f32[8,128]{1,0:T(8,128)S(1)} %copy-done.1, s32[1,16]{1,0:T(1,128)S(1)} %bitcast.1, bf16[1,256]{1,0:T(2,128)(2,1)S(1)} %reshape.15.scale), custom_call_target="tpu_custom_call" | custom-call | tf_op jit(solution)/shard_map/pallas_call | solution.py:214
  25.1 0.6 %copy.11 = f32[1,1,128,128]{3,2,1,0:T(8,128)} copy(f32[1,1,128,128]{3,2,1,0:T(8,128)S(1)} %get-tuple-element.4) | data formatting | bytes 131072
  25.8 0.5 %copy.12 = f32[1,1,128]{2,1,0:T(1,128)} copy(f32[1,1,128]{2,1,0:T(1,128)S(1)} %get-tuple-element.5) | data formatting | bytes 1024
  (1 shorter events, 0.0 us)
Async XLA Ops:
  0.6 0.7 %copy-start.4 = (bf16[256]{0:T(256)(128)(2,1)S(1)}, bf16[256]{0:T(256)(128)(2,1)}, u32[]{:S(2)}) copy-start(bf16[256]{0:T(256)(128)(2,1)} %param.9) | copy-start | bytes 1540
  1.3 0.7 %copy-start.3 = (s32[1,8,2]{1,2,0:T(2,128)S(1)}, s32[1,8,2]{1,2,0:T(2,128)}, u32[]{:S(2)}) copy-start(s32[1,8,2]{1,2,0:T(2,128)} %param.6) | copy-start | bytes 196
  2.0 0.7 %copy-start.1 = (f32[8,128]{1,0:T(8,128)S(1)}, f32[8,128]{1,0:T(8,128)}, u32[]{:S(2)}) copy-start(f32[8,128]{1,0:T(8,128)} %residual.1) | copy-start | bytes 12292
  2.0 0.7 %copy-start.2 = (s32[16]{0:T(128)S(1)}, s32[16]{0:T(128)}, u32[]{:S(2)}) copy-start(s32[16]{0:T(128)} %param.8) | copy-start | bytes 196
  2.7 1.0 %copy-start = (bf16[4,2,2,128,128]{4,3,2,1,0:T(8,128)(2,1)S(1)}, bf16[4,2,2,128,128]{4,3,2,1,0:T(8,128)(2,1)}, u32[]{:S(2)}) copy-start(bf16[4,2,2,128,128]{4,3,2,1,0:T(8,128)(2,1)} %jac.1) | copy-start | bytes 1572868
